TPU v7x, 32 devices: a whole 2x2x4 slice. The times are simulated.
32 devices in a mesh: dp: 8 (over y, x, core), tensor: 4 (over z).
Axes of the slice: x: 2, y: 2, z: 4, core: 2. Of those that a mesh axis runs over, the one named last changes fastest.
Arguments:
- inputs: bfloat16 [16, 1024, 1024], P('dp', None, 'tensor'), may hold values from -6 to 6
- segment: int32 [16, 1024], P('dp'), may hold values from 0 to 4, as said below
- cotangent: bfloat16 [16, 1024, 1024], P('dp', None, 'tensor'), may hold values from -6 to 6
- norm_gain: float32 [1024], replicated, may hold values from 0.1 to 1.9
- weight_z: bfloat16 [1024, 2048], P(None, 'tensor'), may hold values from -0.1875 to 0.1875
- weight_x: bfloat16 [1024, 2048], P(None, 'tensor'), may hold values from -0.1875 to 0.1875
- weight_bc: bfloat16 [1024, 256], replicated, may hold values from -0.1875 to 0.1875
- weight_dt: bfloat16 [1024, 32], P(None, 'tensor'), may hold values from -0.1875 to 0.1875
- conv_weight_x: float32 [4, 2048], P(None, 'tensor'), may hold values from -3 to 3
- conv_bias_x: float32 [2048], P('tensor'), may hold values from -3 to 3
- conv_weight_bc: float32 [4, 256], replicated, may hold values from -3 to 3
- conv_bias_bc: float32 [256], replicated, may hold values from -3 to 3
- step_bias: float32 [32], P('tensor'), may hold values from -6 to -2
- decay_log: float32 [32], P('tensor'), may hold values from 0 to 2.77
- skip_gain: float32 [32], P('tensor'), may hold values from 0.5 to 2
- gate_gain: float32 [2048], P('tensor'), may hold values from 0.1 to 1.9
- weight_out: bfloat16 [2048, 1024], P('tensor'), may hold values from -0.125 to 0.125
Outputs:
- output: bfloat16 [16, 1024, 1024], P('dp', None, 'tensor')
- input_grad: float32 [16, 1024, 1024], P('dp', None, 'tensor')
- norm_gain_grad: float32 [1024], P('tensor')
- weight_z_grad: float32 [1024, 2048], P('dp', 'tensor')
- weight_x_grad: float32 [1024, 2048], P('dp', 'tensor')
- weight_bc_grad: float32 [1024, 256], P('dp')
- weight_dt_grad: float32 [1024, 32], P('dp', 'tensor')
- conv_weight_x_grad: float32 [4, 2048], P(None, 'tensor')
- conv_bias_x_grad: float32 [2048], P('tensor')
- conv_weight_bc_grad: float32 [4, 256], replicated
- conv_bias_bc_grad: float32 [256], replicated
- step_bias_grad: float32 [32], P('tensor')
- decay_log_grad: float32 [32], P('tensor')
- skip_gain_grad: float32 [32], P('tensor')
- gate_gain_grad: float32 [2048], P('tensor')
- weight_out_grad: float32 [2048, 1024], P('tensor', 'dp')
Inputs may be any that keep to these rules, and one draw needn't show every extreme that they name: `segment`: segment numbers start at 0 in each sequence and never fall along it; a new number starts a new document, where the scan state and the convolution restart. Each sequence holds one document of exactly 800 tokens, at its start or at its end; the inner documents have 60 to 800 tokens, the one at the other end may be shorter.
All inputs are finite; a program needn't handle non-finite values.
Results may differ from a plain program's by a relative error of at most 0.008.
Values may be sent and summed in bfloat16 or wider, within the bound.
No kernel may reach another device: no remote copies, remote signals or barrier semaphores. Data moves between devices by JAX's collectives and lax.ppermute only.
A program may use at most 192 MiB of HBM per device.

v0:
```python
import jax
import jax.numpy as jnp
from jax import lax
from jax.sharding import PartitionSpec as P

SPAN = 256
SEQ_MB = 1
INNER = 2048
eps = 1e-05


def causal_conv(values, weights, biases, segment):
    taps = weights.shape[0]
    total = biases + weights[taps - 1] * values
    for offset in range(1, taps):
        moved = jnp.pad(values, ((0, 0), (offset, 0), (0, 0)))[:, :-offset]
        earlier = jnp.pad(segment, ((0, 0), (offset, 0)), constant_values=-1)[:, :-offset]
        same_doc = (earlier == segment).astype(values.dtype)[..., None]
        total = total + weights[taps - 1 - offset] * moved * same_doc
    return total


def ssd_scan(values, decays, deltas, b_matrix, c_matrix, segment, block_len):
    seq_count, length, head_count, head_size = values.shape
    block_count = length // block_len

    def to_blocks(source):
        shaped = source.reshape((seq_count, block_count, block_len) + source.shape[2:])
        return jnp.moveaxis(shaped, 1, 0)

    pieces = tuple(
        (to_blocks(source) for source in (values, decays, deltas, b_matrix, c_matrix, segment))
    )
    state_init = jnp.zeros((seq_count, head_count, b_matrix.shape[-1], head_size), values.dtype)
    prev_init = jnp.full((seq_count,), -1, jnp.int32)
    lower_tri = jnp.arange(block_len)[:, None] >= jnp.arange(block_len)[None, :]

    def advance(carried_in, block_in):
        prior_state, previous = carried_in
        value_blk, decay_blk, delta_blk, b_blk, c_blk, seg_blk = block_in
        cumulative = jnp.cumsum(decay_blk, axis=1)
        allowed = (seg_blk[:, :, None] == seg_blk[:, None, :]) & lower_tri[None]
        masking = allowed.astype(values.dtype)[..., None]
        spread = cumulative[:, :, None, :] - cumulative[:, None, :, :]
        kernel = jnp.exp(jnp.where(allowed[..., None], spread, 0.0)) * masking
        scores = jnp.einsum("stn,sun->stu", c_blk, b_blk, precision=lax.Precision.HIGHEST)
        mixing = scores[..., None] * kernel * delta_blk[:, None, :, :]
        inside = jnp.einsum("stuh,suhp->sthp", mixing, value_blk, precision=lax.Precision.HIGHEST)
        final_seg = seg_blk[:, -1]
        same_end = (seg_blk == final_seg[:, None]).astype(values.dtype)[..., None]
        tail_weight = jnp.exp(cumulative[:, -1:, :] - cumulative) * same_end * delta_blk
        local_state = jnp.einsum(
            "sun,suhp->shnp",
            b_blk,
            tail_weight[..., None] * value_blk,
            precision=lax.Precision.HIGHEST,
        )
        entering = (
            jnp.exp(cumulative) * (seg_blk == previous[:, None]).astype(values.dtype)[..., None]
        )
        outside = (
            jnp.einsum("stn,shnp->sthp", c_blk, prior_state, precision=lax.Precision.HIGHEST)
            * entering[..., None]
        )
        carried = (
            jnp.exp(cumulative[:, -1, :]) * (final_seg == previous).astype(values.dtype)[:, None]
        )
        new_state = carried[:, :, None, None] * prior_state + local_state
        return ((new_state, final_seg), inside + outside)

    _, results = lax.scan(jax.checkpoint(advance), (state_init, prev_init), pieces)
    return jnp.moveaxis(results, 0, 1).reshape(seq_count, length, head_count, head_size)


def mixer(gate_pre, value_pre, bc_pre, delta_pre, params, segment):
    conv_weight_x, conv_bias_x, conv_weight_bc, conv_bias_bc, step_bias, decay_log, skip_gain = (
        params
    )
    conv_value = jax.nn.silu(causal_conv(value_pre, conv_weight_x, conv_bias_x, segment))
    conv_bc = jax.nn.silu(causal_conv(bc_pre, conv_weight_bc, conv_bias_bc, segment))
    state_size = conv_bc.shape[-1] // 2
    deltas = jax.nn.softplus(delta_pre + step_bias)
    decays = -deltas * jnp.exp(decay_log)
    seq_count, length, head_count = deltas.shape
    values = conv_value.reshape(seq_count, length, head_count, -1)
    scan_result = ssd_scan(
        values, decays, deltas, conv_bc[..., :state_size], conv_bc[..., state_size:], segment, SPAN
    )
    scan_result = scan_result + skip_gain[:, None] * values
    return scan_result.reshape(gate_pre.shape) * jax.nn.silu(gate_pre)


def project(left_operand, right_operand):
    return jnp.einsum(
        "ofp,pv->ofv", left_operand, right_operand, preferred_element_type=jnp.float32
    )


def project_back(left_operand, right_operand):
    return jnp.einsum(
        "igh,rh->igr", left_operand, right_operand, preferred_element_type=jnp.float32
    )


def outer_sum(left_operand, right_operand):
    return jnp.einsum(
        "vzq,vza->qa", left_operand, right_operand, preferred_element_type=jnp.float32
    )


def add_tree(left_operand, right_operand):
    return jax.tree.map(jnp.add, left_operand, right_operand)


def per_device(
    inputs,
    segment,
    cotangent,
    norm_gain,
    weight_z,
    weight_x,
    weight_bc,
    weight_dt,
    conv_weight_x,
    conv_bias_x,
    conv_weight_bc,
    conv_bias_bc,
    step_bias,
    decay_log,
    skip_gain,
    gate_gain,
    weight_out,
):
    model_width = weight_z.shape[0]
    share_width = inputs.shape[2]
    share_start = lax.axis_index("tensor") * share_width
    gain_share = lax.dynamic_slice_in_dim(norm_gain, share_start, share_width, 0)
    bc_share = lax.dynamic_slice_in_dim(weight_bc, share_start, share_width, 0)
    params = (
        conv_weight_x,
        conv_bias_x,
        conv_weight_bc,
        conv_bias_bc,
        step_bias,
        decay_log,
        skip_gain,
    )
    big_grads = None
    small_grads = None
    rounds = inputs.shape[0] // SEQ_MB
    outputs = []
    input_grads = []
    for batch_step in range(rounds):
        row_start = batch_step * SEQ_MB
        local_in = inputs[row_start : row_start + SEQ_MB]
        local_seg = segment[row_start : row_start + SEQ_MB]
        local_cot = cotangent[row_start : row_start + SEQ_MB]
        whole_in, cotangent_entire = (
            lax.all_gather(local_in, "tensor", axis=2, tiled=True),
            lax.all_gather(local_cot, "tensor", axis=2, tiled=True),
        )
        residual = whole_in.astype(jnp.float32)
        scale_in = lax.rsqrt(jnp.mean(residual * residual, axis=-1, keepdims=True) + eps)
        normed = (residual * scale_in * norm_gain).astype(jnp.bfloat16)
        gate_pre = project(normed, weight_z)
        value_pre = project(normed, weight_x)
        bc_pre = project(normed, weight_bc)
        delta_pre = project(normed, weight_dt)

        def local_mixer(gate_in, value_in, bc_in, delta_in, param_set):
            return mixer(gate_in, value_in, bc_in, delta_in, param_set, local_seg)

        gated_out, pullback = jax.vjp(local_mixer, gate_pre, value_pre, bc_pre, delta_pre, params)
        d_mixed = project_back(cotangent_entire, weight_out)
        squares, gate_dot = lax.psum(
            (
                jnp.sum(gated_out * gated_out, axis=-1),
                jnp.sum(d_mixed * gate_gain * gated_out, axis=-1),
            ),
            "tensor",
        )
        scale_gate = lax.rsqrt(squares / INNER + eps)[..., None]
        mixer_output = (gated_out * scale_gate * gate_gain).astype(jnp.bfloat16)
        partial_value = project(mixer_output, weight_out)
        summed = lax.psum_scatter(partial_value, "tensor", scatter_dimension=2, tiled=True)
        outputs.append((local_in.astype(jnp.float32) + summed).astype(jnp.bfloat16))
        grad_out = jnp.einsum(
            "mka,mkg->ag", mixer_output, cotangent_entire, preferred_element_type=jnp.float32
        )
        grad_gate_gain = jnp.sum(d_mixed * gated_out * scale_gate, axis=(0, 1))
        d_gated = (
            scale_gate * gate_gain * d_mixed
            - gated_out * scale_gate**3 * (gate_dot / INNER)[..., None]
        )
        d_gate, d_value, d_bc, d_delta, d_params = pullback(d_gated)
        d_bc, d_conv_weight_bc, d_conv_bias_bc = lax.psum(
            (d_bc, d_params[2], d_params[3]), "tensor"
        )
        low_gate = d_gate.astype(jnp.bfloat16)
        low_value = d_value.astype(jnp.bfloat16)
        low_bc = d_bc.astype(jnp.bfloat16)
        low_delta = d_delta.astype(jnp.bfloat16)
        grad_z = outer_sum(normed, low_gate)
        grad_x = outer_sum(normed, low_value)
        grad_bc = outer_sum(normed, low_bc)
        grad_dt = outer_sum(normed, low_delta)
        d_normed = (
            project_back(low_gate, weight_z)
            + project_back(low_value, weight_x)
            + project_back(low_delta, weight_dt)
        )
        bc_term = project_back(low_bc, bc_share)
        shared_input = lax.dynamic_slice_in_dim(residual, share_start, share_width, 2)
        d_share = lax.psum_scatter(d_normed, "tensor", scatter_dimension=2, tiled=True) + bc_term
        norm_dot = lax.psum(jnp.sum(d_share * gain_share * shared_input, axis=-1), "tensor")
        grad_norm_gain = jnp.sum(d_share * shared_input * scale_in, axis=(0, 1))
        input_grads.append(
            local_cot.astype(jnp.float32)
            + scale_in * gain_share * d_share
            - shared_input * scale_in**3 * (norm_dot / model_width)[..., None]
        )
        big_now = (grad_z, grad_x, grad_bc, grad_dt, grad_out)
        small_now = (
            grad_norm_gain,
            d_params[0],
            d_params[1],
            d_conv_weight_bc,
            d_conv_bias_bc,
            d_params[4],
            d_params[5],
            d_params[6],
            grad_gate_gain,
        )
        big_grads = big_now if big_grads is None else add_tree(big_grads, big_now)
        small_grads = small_now if small_grads is None else add_tree(small_grads, small_now)
    output = jnp.concatenate(outputs, axis=0)
    input_grad = jnp.concatenate(input_grads, axis=0)
    big_grads = (
        lax.psum_scatter(big_grads[0], "dp", scatter_dimension=0, tiled=True),
        lax.psum_scatter(big_grads[1], "dp", scatter_dimension=0, tiled=True),
        lax.psum_scatter(big_grads[2], "dp", scatter_dimension=0, tiled=True),
        lax.psum_scatter(big_grads[3], "dp", scatter_dimension=0, tiled=True),
        lax.psum_scatter(big_grads[4], "dp", scatter_dimension=1, tiled=True),
    )
    small_grads = lax.psum(small_grads, "dp")
    return (
        output,
        input_grad,
        small_grads[0],
        big_grads[0],
        big_grads[1],
        big_grads[2],
        big_grads[3],
        small_grads[1],
        small_grads[2],
        small_grads[3],
        small_grads[4],
        small_grads[5],
        small_grads[6],
        small_grads[7],
        small_grads[8],
        big_grads[4],
    )


def solution(mesh):
    return jax.shard_map(
        per_device,
        mesh=mesh,
        in_specs=(
            P("dp", None, "tensor"),
            P("dp", None),
            P("dp", None, "tensor"),
            P(),
            P(None, "tensor"),
            P(None, "tensor"),
            P(),
            P(None, "tensor"),
            P(None, "tensor"),
            P("tensor"),
            P(),
            P(),
            P("tensor"),
            P("tensor"),
            P("tensor"),
            P("tensor"),
            P("tensor", None),
        ),
        out_specs=(
            P("dp", None, "tensor"),
            P("dp", None, "tensor"),
            P("tensor"),
            P("dp", "tensor"),
            P("dp", "tensor"),
            P("dp", None),
            P("dp", "tensor"),
            P(None, "tensor"),
            P("tensor"),
            P(),
            P(),
            P("tensor"),
            P("tensor"),
            P("tensor"),
            P("tensor"),
            P("tensor", "dp"),
        ),
        check_vma=False,
    )
```

profile of v0, /device:TPU:0, one launch (start us, length us, event | category | flops | bytes accessed | tf_op | source)
XLA Modules:
  0.0 1255.8 jit_solution(11214322786182025757)
XLA Ops:
  14.4 44.7 %all-gather.5.cloned.1.call-done = bf16[1,1024,1024]{2,1,0:T(8,128)(2,1)} async-done(((bf16[1,1024,256]{2,1,0:T(8,128)(2,1)}), bf16[1,1024,1024]{2,1,0:T(8,128)(2,1)}) %all-gather.5.cloned.1.call-update) | async-done | bytes 2097168 | tf_op jit(solution)/shard_map/all_gather | solution.py:159
  62.0 43.8 %all-gather.7.cloned.1.call-done = bf16[1,1024,1024]{2,1,0:T(8,128)(2,1)} async-done(((bf16[1,1024,256]{2,1,0:T(8,128)(2,1)}), bf16[1,1024,1024]{2,1,0:T(8,128)(2,1)}) %all-gather.7.cloned.1.call-update) | async-done | bytes 2097168 | tf_op jit(solution)/shard_map/all_gather | solution.py:159
  123.0 5.0 fusion.299
  128.0 4.9 reshape.2758
  132.9 3.8 copy.200
  140.0 58.6 %while.91 = (s32[]{:T(128)}, f32[1,8,128,64]{2,3,1,0:T(8,128)}, s32[1]{0:T(128)}, f32[4,1,256,8,64]{2,4,3,1,0:T(8,128)}, f32[4,1,8,128,64]{3,4,2,1,0:T(8,128)}, ...) while((s32[]{:T(128)}, f32[1,8,128,64]{2,3,1,0:T(8,128)}, ...), condition=%wide.region_12.14_spmd.clone, body=%wide.region_9.13_spmd.clone.sunk | while | flops 909716480 | bytes 14458493 | solution.py:71
  145.9 3.4 fusion.566
  160.8 3.4 fusion.566
  198.6 4.0 copy.230
  202.6 4.8 reshape.2752
  209.6 4.4 reshape.2757
  214.0 3.8 copy.192
  220.5 58.8 %while.90 = (s32[]{:T(128)}, f32[1,8,128,64]{2,3,1,0:T(8,128)}, s32[1]{0:T(128)}, f32[4,1,256,8,64]{2,4,3,1,0:T(8,128)}, f32[4,1,8,128,64]{3,4,2,1,0:T(8,128)}, ...) while((s32[]{:T(128)}, f32[1,8,128,64]{2,3,1,0:T(8,128)}, ...), condition=%wide.region_4.6_spmd.clone, body=%wide.region_1.5_spmd.clone.sunk | while | flops 909716480 | bytes 14458309 | solution.py:71
  279.3 3.8 copy.229
  283.1 4.8 reshape.2751
  292.1 4.8 multiply_reduce_fusion.23
  296.8 9.4 all-reduce.58
  306.4 4.4 fusion.284
  310.8 7.2 multiply_reduce_fusion.11
  318.0 9.8 all-reduce.57
  328.0 8.7 fusion.281
  340.1 4.7 fusion.270
  344.8 4.4 reshape.2753
  349.2 3.8 copy.212
  357.4 126.8 %while.92 = (s32[]{:T(128)}, f32[1,8,128,64]{2,3,1,0:T(8,128)S(1)}, f32[4,1,256,8,64]{2,4,3,1,0:T(8,128)}, f32[4,1,256,8]{2,3,1,0:T(8,128)}, f32[4,1,256,8]{2,3,...) while((s32[]{:T(128)}, f32[1,8,128,64]{2,3,1,0:T(8,128)S(1)}, ...), condition=%wide.region_31.33_spmd.clone, body=%wide.region_18.32_spmd.clone.sunk | while | flops 2126752768 | bytes 21947920 | solution.py:71
  367.5 4.2 fusion.588
  384.8 3.9 fusion.592
  399.1 4.2 fusion.588
  416.4 4.0 fusion.592
  430.7 4.2 fusion.588
  448.0 4.0 fusion.592
  462.3 4.2 fusion.588
  479.6 4.0 fusion.592
  484.2 4.4 reshape.2755
  488.6 3.8 copy.223
  496.9 128.2 %while.93 = (s32[]{:T(128)}, f32[1,8,128,64]{2,3,1,0:T(8,128)S(1)}, f32[4,1,256,8,64]{2,4,3,1,0:T(8,128)}, f32[4,1,256,8]{2,3,1,0:T(8,128)}, f32[4,1,256,8]{2,3,...) while((s32[]{:T(128)}, f32[1,8,128,64]{2,3,1,0:T(8,128)S(1)}, ...), condition=%wide.region_51.53_spmd.clone, body=%wide.region_38.52_spmd.clone.sunk | while | flops 2126752768 | bytes 20604208 | solution.py:71
  507.3 4.1 fusion.616
  524.6 3.9 fusion.620
  539.3 4.1 fusion.616
  556.6 3.9 fusion.620
  571.3 4.1 fusion.616
  588.6 3.9 fusion.620
  603.4 4.1 fusion.616
  620.6 3.9 fusion.620
  625.1 3.8 copy.233
  629.0 4.9 reshape.2754
  633.9 8.2 multiply_reduce_fusion.19
  642.1 3.8 copy.236
  645.9 4.9 reshape.2756
  650.9 6.6 multiply_reduce_fusion.15
  677.4 4.4 convolution_bitcast_fusion.12
  683.5 4.5 convolution_bitcast_fusion.13
  698.8 130.9 %all-reduce.60 = (bf16[1,1024,256]{2,1,0:T(8,128)(2,1)}, bf16[1,1024,256]{2,1,0:T(8,128)(2,1)}) all-reduce(f32[1,1024,256]{2,1,0:T(8,128)} %get-tuple-element.1710, f32[1,1024,256]{2,1,0:T(8,128)} %get-tuple-element.1709), channel_id=1, replica_groups=mesh['dp'=8,'tensor'=4] {'tensor'}, use_global_device_ids=true, to_apply=%region_53.55 | all-reduce | flops 524288 | bytes 3145728 | tf_op jit(solution)/shard_map/psum | solution.py:196
  836.3 3.7 fusion.282
  863.2 15.0 %reduce-scatter.14.cloned.1.call-done = f32[1,1024,256]{2,1,0:T(8,128)} async-done(((f32[1,1024,1024]{2,1,0:T(8,128)}), f32[1,1024,256]{2,1,0:T(8,128)}) %reduce-scatter.14.cloned.1.call-update) | async-done | bytes 1048592 | tf_op jit(solution)/shard_map/reduce_scatter | solution.py:214
  881.1 18.4 %all-reduce.55 = (f32[1,1024]{1,0:T(1,128)S(1)}, f32[1,1024]{1,0:T(1,128)S(1)}, f32[4,256]{1,0:T(4,128)S(1)}, f32[256]{0:T(256)S(1)}) all-reduce(f32[1,1024]{1,0:T(1,128)S(1)} %bitcast.1481, f32[1,1024]{1,0:T(1,128)S(1)} %bitcast.1480, f32[4,256]{1,0:T(4,128)S(1)} %add_add_fusion.1, ...), channel_id=1, replica_groups=mesh['dp'=8,'tensor'=4] {'tensor'}, use_global_device_ids=true, to_apply=%region_55.57 | all-reduce | flops 3328 | bytes 26624 | tf_op jit(solution)/shard_map/psum | solution.py:215
  899.5 24.6 %all-reduce.54 = (f32[256]{0:T(256)}, f32[4,512]{1,0:T(4,128)}, f32[512]{0:T(512)}, f32[4,256]{1,0:T(4,128)}, f32[256]{0:T(256)}, /*index=5*/f32[8]{0:T(128)}, f32[8]{0:T(128)}, f32[8]{0:T(128)}, f32[512]{0:T(512)}) all-reduce(f32[256]{0:T(256)S(1)} %add.531, ...), channel_id=1, replica_groups=mesh['dp'=8,'tensor'=4] {'dp'}, use_global_device_ids=true, to_apply=%region_58.60 | all-reduce | flops 4632 | bytes 37056 | tf_op jit(solution)/shard_map/psum | solution.py:245
  924.1 34.1 %reduce-scatter.12.cloned.1.call-done = f32[1,1024,256]{2,1,0:T(8,128)} async-done(((f32[1,1024,1024]{2,1,0:T(8,128)}), f32[1,1024,256]{2,1,0:T(8,128)}) %reduce-scatter.12.cloned.1.call-update) | async-done | bytes 1048592 | tf_op jit(solution)/shard_map/reduce_scatter | solution.py:185
  958.2 79.6 %reduce-scatter.10.cloned.1.call-done = f32[1,1024,256]{2,1,0:T(8,128)} async-done(((f32[1,1024,1024]{2,1,0:T(8,128)}), f32[1,1024,256]{2,1,0:T(8,128)}) %reduce-scatter.10.cloned.1.call-update) | async-done | bytes 1048592 | tf_op jit(solution)/shard_map/reduce_scatter | solution.py:185
  1045.4 27.8 %reduce-scatter.24.cloned.1.call-done = f32[128,8]{0,1:T(8,128)} async-done(((f32[1024,8]{0,1:T(8,128)}), f32[128,8]{0,1:T(8,128)}) %reduce-scatter.24.cloned.1.call-update) | async-done | bytes 4112 | tf_op jit(solution)/shard_map/reduce_scatter | solution.py:242
  1073.1 40.0 %reduce-scatter.22.cloned.1.call-done = f32[128,256]{1,0:T(8,128)} async-done(((f32[1024,256]{1,0:T(8,128)}), f32[128,256]{1,0:T(8,128)}) %reduce-scatter.22.cloned.1.call-update) | async-done | bytes 131088 | tf_op jit(solution)/shard_map/reduce_scatter | solution.py:241
  1113.2 45.5 %reduce-scatter.26.cloned.1.call-done = f32[512,128]{1,0:T(8,128)} async-done(((f32[512,1024]{1,0:T(8,128)}), f32[512,128]{1,0:T(8,128)}) %reduce-scatter.26.cloned.1.call-update) | async-done | bytes 262160 | tf_op jit(solution)/shard_map/reduce_scatter | solution.py:243
  1158.6 45.0 %reduce-scatter.20.cloned.1.call-done = f32[128,512]{1,0:T(8,128)} async-done(((f32[1024,512]{1,0:T(8,128)}), f32[128,512]{1,0:T(8,128)}) %reduce-scatter.20.cloned.1.call-update) | async-done | bytes 262160 | tf_op jit(solution)/shard_map/reduce_scatter | solution.py:240
  1203.6 45.5 %reduce-scatter.18.cloned.1.call-done = f32[128,512]{1,0:T(8,128)} async-done(((f32[1024,512]{1,0:T(8,128)}), f32[128,512]{1,0:T(8,128)}) %reduce-scatter.18.cloned.1.call-update) | async-done | bytes 262160 | tf_op jit(solution)/shard_map/reduce_scatter | solution.py:239
  (1137 shorter events, 400.3 us)
Async XLA Ops:
  7.2 280.7 %copy-start = (bf16[1024,512]{1,0:T(8,128)(2,1)S(1)}, bf16[1024,512]{1,0:T(8,128)(2,1)}, u32[]{:S(2)}) copy-start(bf16[1024,512]{1,0:T(8,128)(2,1)} %param.30) | copy-start | bytes 3145732
  7.2 51.9 %all-gather.5.cloned.1.call-start = ((), (), s32[]{:S(2)}) async-start(), calls=%async_computation.9 | async-start | bytes 2621440 | tf_op jit(solution)/shard_map/all_gather | solution.py:159
  9.7 96.1 %all-gather.7.cloned.1.call-start = ((), (), s32[]{:S(2)}) async-start(), calls=%async_computation.11 | async-start | bytes 2621440 | tf_op jit(solution)/shard_map/all_gather | solution.py:159
  10.4 296.0 %all-gather.11.cloned.1.call-start = ((), (), s32[]{:S(2)}) async-start(), calls=%async_computation.15 | async-start | bytes 2621440 | tf_op jit(solution)/shard_map/all_gather | solution.py:160
  11.6 299.3 %all-gather.9.cloned.1.call-start = ((), (), s32[]{:S(2)}) async-start(), calls=%async_computation.13 | async-start | bytes 2621440 | tf_op jit(solution)/shard_map/all_gather | solution.py:160
  12.1 849.4 %reduce-scatter.16.cloned.1.call-start = ((), (), s32[]{:S(2)}) async-start(), calls=%async_computation.16 | async-start | bytes 5242880 | tf_op jit(solution)/shard_map/reduce_scatter | solution.py:214
  13.5 109.5 %copy-start.113 = (f32[1,512]{1,0:T(1,128)}, f32[1,512]{1,0:T(1,128)S(1)}, u32[]{:S(2)}) copy-start(f32[1,512]{1,0:T(1,128)S(1)} %get-tuple-element.1669) | copy-start | bytes 6148
  13.5 109.5 %copy-start.115 = (f32[1,512]{1,0:T(1,128)}, f32[1,512]{1,0:T(1,128)S(1)}, u32[]{:S(2)}) copy-start(f32[1,512]{1,0:T(1,128)S(1)} %get-tuple-element.1670) | copy-start | bytes 6148
  13.5 101.8 %copy-start.138 = (f32[8]{0:T(128)}, f32[8]{0:T(128)S(1)}, u32[]{:S(2)}) copy-start(f32[8]{0:T(128)S(1)} %exp.270) | copy-start | bytes 100
  14.3 108.6 %copy-start.79 = (f32[1,1024]{1,0:T(1,128)}, f32[1,1024]{1,0:T(1,128)S(1)}, u32[]{:S(2)}) copy-start(f32[1,1024]{1,0:T(1,128)S(1)} %get-tuple-element.1693) | copy-start | bytes 12292
  14.4 108.6 %copy-start.81 = (f32[1,1024]{1,0:T(1,128)}, f32[1,1024]{1,0:T(1,128)S(1)}, u32[]{:S(2)}) copy-start(f32[1,1024]{1,0:T(1,128)S(1)} %get-tuple-element.1694) | copy-start | bytes 12292
  14.4 108.6 %copy-start.83 = (f32[1,1024]{1,0:T(1,128)}, f32[1,1024]{1,0:T(1,128)S(1)}, u32[]{:S(2)}) copy-start(f32[1,1024]{1,0:T(1,128)S(1)} %get-tuple-element.1695) | copy-start | bytes 12292
  14.4 108.6 %copy-start.85 = (f32[1,1024]{1,0:T(1,128)}, f32[1,1024]{1,0:T(1,128)S(1)}, u32[]{:S(2)}) copy-start(f32[1,1024]{1,0:T(1,128)S(1)} %get-tuple-element.1719) | copy-start | bytes 12292
  14.4 108.6 %copy-start.87 = (f32[1,1024]{1,0:T(1,128)}, f32[1,1024]{1,0:T(1,128)S(1)}, u32[]{:S(2)}) copy-start(f32[1,1024]{1,0:T(1,128)S(1)} %get-tuple-element.1720) | copy-start | bytes 12292
  14.4 108.6 %copy-start.89 = (f32[1,1024]{1,0:T(1,128)}, f32[1,1024]{1,0:T(1,128)S(1)}, u32[]{:S(2)}) copy-start(f32[1,1024]{1,0:T(1,128)S(1)} %get-tuple-element.1721) | copy-start | bytes 12292
  14.4 94.2 %copy-start.137 = (f32[1024]{0:T(1024)S(1)}, f32[1024]{0:T(1024)}, u32[]{:S(2)}) copy-start(f32[1024]{0:T(1024)} %param.29) | copy-start | bytes 12292
  59.1 49.5 %copy-start.10 = (bf16[1,1024,1024]{2,1,0:T(8,128)(2,1)S(1)}, bf16[1,1024,1024]{2,1,0:T(8,128)(2,1)}, u32[]{:S(2)}) copy-start(bf16[1,1024,1024]{2,1,0:T(8,128)(2,1)} %all-gather.5.cloned.1.call-done) | copy-start | bytes 6291460
  62.0 47.9 %copy-start.105 = (f32[1024]{0:T(1024)}, f32[1024]{0:T(1024)S(1)}, u32[]{:S(2)}) copy-start(f32[1024]{0:T(1024)S(1)} %get-tuple-element.1679) | copy-start | bytes 12292
  114.0 9.0 copy-start.7
  128.0 208.7 %copy-start.1 = (f32[1,1024,512]{2,1,0:T(8,128)}, f32[1,1024,512]{2,1,0:T(8,128)S(1)}, u32[]{:S(2)}) copy-start(f32[1,1024,512]{2,1,0:T(8,128)S(1)} %get-tuple-element.1666) | copy-start | bytes 6291460
  306.3 30.4 %copy-start.103 = (f32[1,1024]{1,0:T(1,128)}, f32[1,1024]{1,0:T(1,128)S(1)}, u32[]{:S(2)}) copy-start(f32[1,1024]{1,0:T(1,128)S(1)} %add_rsqrt_fusion) | copy-start | bytes 12292
  306.3 30.4 %copy-start.101 = (f32[1,1024]{1,0:T(1,128)}, f32[1,1024]{1,0:T(1,128)S(1)}, u32[]{:S(2)}) copy-start(f32[1,1024]{1,0:T(1,128)S(1)} %add_rsqrt_fusion.2) | copy-start | bytes 12292
  327.9 9.2 copy-start.24
  327.9 9.8 copy-start.25
  327.9 10.4 copy-start.32
  327.9 11.0 copy-start.34
  328.0 11.6 copy-start.36
  328.0 12.2 copy-start.37
  357.8 9.0 copy-start.65
  360.9 10.8 copy-start.50
  375.8 9.0 copy-start.40
  375.8 9.0 copy-start.55
  389.4 9.0 copy-start.65
  392.4 10.8 copy-start.50
  407.4 9.0 copy-start.40
  407.4 9.0 copy-start.55
  421.0 9.0 copy-start.65
  424.1 10.8 copy-start.50
  439.0 9.0 copy-start.40
  439.0 9.0 copy-start.55
  452.6 9.0 copy-start.65
  455.7 10.8 copy-start.50
  470.6 9.0 copy-start.40
  470.6 9.0 copy-start.55
  500.1 11.3 copy-start.52
  515.6 9.0 copy-start.43
  515.6 9.0 copy-start.57
  532.1 11.4 copy-start.52
  547.6 9.0 copy-start.43
  564.1 11.4 copy-start.52
  579.6 9.0 copy-start.43
  596.1 11.4 copy-start.52
  611.7 9.0 copy-start.43
  611.7 9.0 copy-start.57
  668.0 210.1 %reduce-scatter.14.cloned.1.call-start = ((), (), s32[]{:S(2)}) async-start(), calls=%async_computation.14 | async-start | bytes 5242880 | tf_op jit(solution)/shard_map/reduce_scatter | solution.py:214
  675.9 282.3 %reduce-scatter.12.cloned.1.call-start = ((), (), s32[]{:S(2)}) async-start(), calls=%async_computation.12 | async-start | bytes 5242880 | tf_op jit(solution)/shard_map/reduce_scatter | solution.py:185
  681.9 355.9 %reduce-scatter.10.cloned.1.call-start = ((), (), s32[]{:S(2)}) async-start(), calls=%async_computation.10 | async-start | bytes 5242880 | tf_op jit(solution)/shard_map/reduce_scatter | solution.py:185
  688.0 385.1 %reduce-scatter.24.cloned.1.call-start = ((), (), s32[]{:S(2)}) async-start(), calls=%async_computation.20 | async-start | bytes 36864 | tf_op jit(solution)/shard_map/reduce_scatter | solution.py:242
  833.1 280.1 %reduce-scatter.22.cloned.1.call-start = ((), (), s32[]{:S(2)}) async-start(), calls=%async_computation.19 | async-start | bytes 1179648 | tf_op jit(solution)/shard_map/reduce_scatter | solution.py:241
  836.3 322.4 %reduce-scatter.26.cloned.1.call-start = ((), (), s32[]{:S(2)}) async-start(), calls=%async_computation.21 | async-start | bytes 2359296 | tf_op jit(solution)/shard_map/reduce_scatter | solution.py:243
  842.8 360.8 %reduce-scatter.20.cloned.1.call-start = ((), (), s32[]{:S(2)}) async-start(), calls=%async_computation.18 | async-start | bytes 2359296 | tf_op jit(solution)/shard_map/reduce_scatter | solution.py:240
  848.8 400.3 %reduce-scatter.18.cloned.1.call-start = ((), (), s32[]{:S(2)}) async-start(), calls=%async_computation.17 | async-start | bytes 2359296 | tf_op jit(solution)/shard_map/reduce_scatter | solution.py:239
  861.4 16.7 %copy-start.106 = (f32[1024]{0:T(1024)S(1)}, f32[1024]{0:T(1024)}, u32[]{:S(2)}) copy-start(f32[1024]{0:T(1024)} %copy-done.105) | copy-start | bytes 12292
  861.4 16.7 %copy-start.108 = (f32[1024]{0:T(1024)S(1)}, f32[1024]{0:T(1024)}, u32[]{:S(2)}) copy-start(f32[1024]{0:T(1024)} %copy-done.107) | copy-start | bytes 12292
  (200 other events, 801.2 us)
Sparse Core Ops, SparseCore 0:
  10.2 48.9 all-gather.4
  61.3 44.4 all-gather.6
  107.4 44.4 all-gather.10
  153.3 44.4 all-gather.8
  668.1 112.7 reduce-scatter.15
  783.1 94.9 reduce-scatter.13
  880.4 77.7 reduce-scatter.11
  960.6 77.1 reduce-scatter.9
  1041.4 31.7 reduce-scatter.23
  1077.1 36.0 reduce-scatter.21
  1117.4 41.2 reduce-scatter.25
  1162.3 41.2 reduce-scatter.19
  1207.8 41.2 reduce-scatter.17
where the time goes:
time: 1270 us; the launch traced here: 1260 us
  waiting for transfers between devices  422 us (33%)
  matrix products  258 us (20%)
  blocking collectives  193 us (15%)
  local copies, waits for them, and re-layouts  173 us (14%)
  other arithmetic  169 us (13%)
  loops' own time  24.3 us (2%)
  between operations  15.6 us (1%)
    psum x1, blocking collectives, per_device(): lax.psum((d_bc, d_params[2], d_params[3]), 'tensor')  131 us
    reduce_scatter x2, waiting for transfers between devices, per_device(): lax.psum_scatter(partial_value, 'tensor', scatter_dimension=2, tiled=True)  114 us
    dot_general x24, matrix products, advance(): jnp.einsum('stuh,suhp->sthp', mixing, value_blk, precision=lax.Precision....  91.5 us
    all_gather x2, waiting for transfers between devices, per_device(): lax.all_gather(local_in, 'tensor', axis=2, tiled=True)  88.5 us
    reduce_scatter x1, waiting for transfers between devices, per_device(): lax.psum_scatter(big_grads[4], 'dp', scatter_dimension=1, tiled=True)  45.5 us
    reduce_scatter x1, waiting for transfers between devices, per_device(): lax.psum_scatter(big_grads[0], 'dp', scatter_dimension=0, tiled=True)  45.5 us
    reduce_scatter x1, waiting for transfers between devices, per_device(): lax.psum_scatter(big_grads[1], 'dp', scatter_dimension=0, tiled=True)  45 us
    reduce_scatter x1, waiting for transfers between devices, per_device(): lax.psum_scatter(big_grads[2], 'dp', scatter_dimension=0, tiled=True)  40 us
  transfers between devices with their start and end apart: 13, of which 10 were waited for; matrix products, arithmetic and copies ran while one was open for 20% of the time, Pallas kernels for 0%

commit v1 on v0

--- a/solution.py
+++ b/solution.py
@@ -7,6 +7,24 @@
 SEQ_MB = 1
 INNER = 2048
 eps = 1e-05
+
+
+def gather_around(array, axis, dim):
+    ways, here, step = (lax.axis_size(axis), lax.axis_index(axis), array.shape[dim])
+    shape = [n * ways if d == dim else n for d, n in enumerate(array.shape)]
+    full = lax.dynamic_update_slice_in_dim(
+        jnp.zeros(shape, array.dtype), array, here * step, axis=dim
+    )
+    going_up = going_down = array
+    for far in range(1, ways // 2 + 1):
+        going_up = lax.ppermute(going_up, axis, [(d, (d + 1) % ways) for d in range(ways)])
+        full = lax.dynamic_update_slice_in_dim(full, going_up, (here - far) % ways * step, axis=dim)
+        if 2 * far < ways:
+            going_down = lax.ppermute(going_down, axis, [(d, (d - 1) % ways) for d in range(ways)])
+            full = lax.dynamic_update_slice_in_dim(
+                full, going_down, (here + far) % ways * step, axis=dim
+            )
+    return full
 
 
 def causal_conv(values, weights, biases, segment):
@@ -156,7 +174,7 @@
         local_seg = segment[row_start : row_start + SEQ_MB]
         local_cot = cotangent[row_start : row_start + SEQ_MB]
         whole_in, cotangent_entire = (
-            lax.all_gather(local_in, "tensor", axis=2, tiled=True),
+            gather_around(local_in, "tensor", 2),
             lax.all_gather(local_cot, "tensor", axis=2, tiled=True),
         )
         residual = whole_in.astype(jnp.float32)

time: 1270 us -> 1160 us (0.913)
  waiting for transfers between devices: 422 us -> 247 us
  starting transfers between devices: 1.11 us -> 43.5 us
  local copies, waits for them, and re-layouts: 173 us -> 201 us
    reduce_scatter x2, waiting for transfers between devices: 114 us -> 0.04 us  [per_device(): lax.psum_scatter(partial_value, 'tensor', scatter_dimension=2, tiled=True)]
    all_gather x2 -> x0, waiting for transfers between devices: 88.5 us -> none  [per_device(): lax.all_gather(local_in, 'tensor', axis=2, tiled=True)]
    ppermute x0 -> x6, waiting for transfers between devices: none -> 54.4 us  [the longest x4 50.9 us: gather_around(): lax.ppermute(going_up, axis, [(d, (d + 1) % ways) for d in range(ways)])]
    ppermute x0 -> x6, starting transfers between devices: none -> 42.7 us  [the longest x4 36.8 us: gather_around(): lax.ppermute(going_up, axis, [(d, (d + 1) % ways) for d in range(ways)])]
    reduce_scatter x1, waiting for transfers between devices: 27.8 us -> 0.01 us  [per_device(): lax.psum_scatter(big_grads[3], 'dp', scatter_dimension=0, tiled=True)]
    reduce_scatter x2, waiting for transfers between devices: 15 us -> 29.1 us  [per_device(): lax.psum_scatter(d_normed, 'tensor', scatter_dimension=2, tiled=True)]
    unnamed x250 -> x258, local copies, waits for them, and re-layouts: 28.7 us -> 26.3 us
  transfers between devices with their start and end apart: 13 -> 17, of which waited for: 10 -> 10; matrix products, arithmetic and copies ran while one was open for 20% -> 53% of each run, Pallas kernels for 0% -> 0%
where the time goes in v1:
time: 1160 us
  matrix products  249 us (21%)
  waiting for transfers between devices  247 us (21%)
  local copies, waits for them, and re-layouts  201 us (17%)
  blocking collectives  195 us (17%)
  other arithmetic  180 us (16%)
  starting transfers between devices  43.5 us (4%)
  loops' own time  24.1 us (2%)
  between operations  16 us (1%)
    psum x1, blocking collectives, per_device(): lax.psum((d_bc, d_params[2], d_params[3]), 'tensor')  125 us
    dot_general x24, matrix products, advance(): jnp.einsum('stuh,suhp->sthp', mixing, value_blk, precision=lax.Precision....  90.6 us
    ppermute x4, waiting for transfers between devices, gather_around(): lax.ppermute(going_up, axis, [(d, (d + 1) % ways) for d in range(ways)])  50.9 us
    another operation x57, other arithmetic  49.8 us
    reduce_scatter x1, waiting for transfers between devices, per_device(): lax.psum_scatter(big_grads[0], 'dp', scatter_dimension=0, tiled=True)  45.5 us
    reduce_scatter x1, waiting for transfers between devices, per_device(): lax.psum_scatter(big_grads[4], 'dp', scatter_dimension=1, tiled=True)  45.5 us
    reduce_scatter x1, waiting for transfers between devices, per_device(): lax.psum_scatter(big_grads[1], 'dp', scatter_dimension=0, tiled=True)  45 us
    ppermute x4, starting transfers between devices, gather_around(): lax.ppermute(going_up, axis, [(d, (d + 1) % ways) for d in range(ways)])  36.8 us
  transfers between devices with their start and end apart: 17, of which 10 were waited for; matrix products, arithmetic and copies ran while one was open for 53% of the time, Pallas kernels for 0%

profile of v1, /device:TPU:0, one launch (start us, length us, event | category | flops | bytes accessed | tf_op | source)
XLA Modules:
  0.0 1156.1 jit_solution(3807847826851456578)
XLA Ops:
  17.3 3.8 collective-permute-start.1
  25.3 10.2 collective-permute-done.3
  35.6 20.0 %collective-permute-start.5 = (bf16[1,1024,256]{2,1,0:T(8,128)(2,1)}, bf16[1,1024,256]{2,1,0:T(8,128)(2,1)}, u32[]{:S(2)}, u32[]{:S(2)}) collective-permute-start(bf16[1,1024,256]{2,1,0:T(8,128)(2,1)} %collective-permute-done.3), channel_id=1, source_target_pairs={{0,1},{1,2},{2,3},{3,0},{4,5},{5,6},{6,7},{7,4},{8,9},{9,10},{10,1... | collective-permute-start | bytes 1572872 | tf_op jit(solution)/shard_map/ppermute | solution.py:20
  55.9 18.9 %collective-permute-done = bf16[1,1024,256]{2,1,0:T(8,128)(2,1)} collective-permute-done((bf16[1,1024,256]{2,1,0:T(8,128)(2,1)}, bf16[1,1024,256]{2,1,0:T(8,128)(2,1)}, u32[]{:S(2)}, u32[]{:S(2)}) %collective-permute-start) | collective-permute-done | bytes 524320 | tf_op jit(solution)/shard_map/ppermute | solution.py:20
  74.8 13.7 %collective-permute-start.2 = (bf16[1,1024,256]{2,1,0:T(8,128)(2,1)}, bf16[1,1024,256]{2,1,0:T(8,128)(2,1)S(1)}, u32[]{:S(2)}, u32[]{:S(2)}) collective-permute-start(bf16[1,1024,256]{2,1,0:T(8,128)(2,1)} %collective-permute-done), channel_id=1, source_target_pairs={{0,1},{1,2},{2,3},{3,0},{4,5},{5,6},{6,7},{7,4},{8,9},{9,10},{10,1... | collective-permute-start | bytes 1572872 | tf_op jit(solution)/shard_map/ppermute | solution.py:20
  93.5 3.6 collective-permute-done.1
  98.2 10.8 collective-permute-done.5
  113.7 10.9 collective-permute-done.2
  142.1 5.0 fusion.299
  147.1 4.9 reshape.2758
  152.0 3.8 copy.200
  159.0 74.6 %while.91 = (s32[]{:T(128)}, f32[1,8,128,64]{2,3,1,0:T(8,128)}, s32[1]{0:T(128)}, f32[4,1,256,8,64]{2,4,3,1,0:T(8,128)}, f32[4,1,8,128,64]{3,4,2,1,0:T(8,128)}, ...) while((s32[]{:T(128)}, f32[1,8,128,64]{2,3,1,0:T(8,128)}, ...), condition=%wide.region_12.14_spmd.clone, body=%wide.region_9.13_spmd.clone.sunk | while | flops 909716480 | bytes 14458309 | solution.py:89
  236.0 4.5 reshape.2757
  240.5 3.8 copy.192
  247.0 50.1 %while.90 = (s32[]{:T(128)}, f32[1,8,128,64]{2,3,1,0:T(8,128)S(1)}, s32[1]{0:T(128)}, f32[4,1,256,8,64]{2,4,3,1,0:T(8,128)}, f32[4,1,8,128,64]{3,4,2,1,0:T(8,128...) while((s32[]{:T(128)}, f32[1,8,128,64]{2,3,1,0:T(8,128)S(1)}, ...), condition=%wide.region_4.6_spmd.clone, body=%wide.region_1.5_spmd.clone.sunk | while | flops 909716480 | bytes 14458309 | solution.py:89
  297.1 3.8 copy.230
  300.9 4.8 reshape.2752
  305.7 3.8 copy.229
  309.5 4.8 reshape.2751
  318.6 4.8 multiply_reduce_fusion.23
  323.3 18.3 %all-reduce.58 = (f32[1,1024]{1,0:T(1,128)S(1)}, f32[1,1024]{1,0:T(1,128)S(1)}) all-reduce(f32[1,1024]{1,0:T(1,128)S(1)} %bitcast.1498, f32[1,1024]{1,0:T(1,128)S(1)} %bitcast.1497), channel_id=1, replica_groups=mesh['dp'=8,'tensor'=4] {'tensor'}, use_global_device_ids=true, to_apply=%region_14.16 | all-reduce | flops 2048 | bytes 16384 | tf_op jit(solution)/shard_map/psum | solution.py:193
  341.7 5.1 convolution_bitcast_fusion.12
  347.2 5.1 convolution_bitcast_fusion.13
  352.4 4.8 fusion.284
  357.2 7.2 multiply_reduce_fusion.11
  364.4 11.9 %all-reduce.57 = (f32[1,1024]{1,0:T(1,128)S(1)}, f32[1,1024]{1,0:T(1,128)S(1)}) all-reduce(f32[1,1024]{1,0:T(1,128)S(1)} %bitcast.1480, f32[1,1024]{1,0:T(1,128)S(1)} %bitcast.1479), channel_id=1, replica_groups=mesh['dp'=8,'tensor'=4] {'tensor'}, use_global_device_ids=true, to_apply=%region_37.39 | all-reduce | flops 2048 | bytes 16384 | tf_op jit(solution)/shard_map/psum | solution.py:193
  376.4 8.5 fusion.281
  385.0 4.4 reshape.2753
  389.3 3.8 copy.212
  397.5 132.8 %while.92 = (s32[]{:T(128)}, f32[1,8,128,64]{2,3,1,0:T(8,128)S(1)}, f32[4,1,256,8,64]{2,4,3,1,0:T(8,128)}, f32[4,1,256,8]{2,3,1,0:T(8,128)}, f32[4,1,256,8]{2,3,...) while((s32[]{:T(128)}, f32[1,8,128,64]{2,3,1,0:T(8,128)S(1)}, ...), condition=%wide.region_31.33_spmd.clone, body=%wide.region_18.32_spmd.clone.sunk | while | flops 2126752768 | bytes 22006084 | solution.py:89
  407.0 4.2 fusion.588
  426.6 3.8 fusion.592
  440.2 4.2 fusion.588
  459.8 3.8 fusion.592
  473.3 4.2 fusion.588
  492.8 3.8 fusion.592
  506.4 4.2 fusion.588
  525.9 3.8 fusion.592
  530.4 4.4 reshape.2755
  534.8 3.8 copy.223
  543.1 140.3 %while.93 = (s32[]{:T(128)}, f32[1,8,128,64]{2,3,1,0:T(8,128)S(1)}, f32[4,1,256,8,64]{2,4,3,1,0:T(8,128)}, f32[4,1,256,8]{2,3,1,0:T(8,128)}, f32[4,1,256,8]{2,3,...) while((s32[]{:T(128)}, f32[1,8,128,64]{2,3,1,0:T(8,128)S(1)}, ...), condition=%wide.region_51.53_spmd.clone, body=%wide.region_38.52_spmd.clone.sunk | while | flops 2126752768 | bytes 21448676 | solution.py:89
  554.3 4.2 fusion.616
  573.9 3.8 fusion.620
  589.3 4.2 fusion.616
  608.9 3.8 fusion.620
  624.3 4.2 fusion.616
  643.9 3.8 fusion.620
  659.4 4.2 fusion.616
  679.0 3.8 fusion.620
  683.4 3.8 copy.233
  687.2 5.0 reshape.2754
  695.2 5.0 reshape.2756
  700.6 6.3 multiply_reduce_fusion.19
  718.9 4.5 fusion.270
  746.9 124.7 %all-reduce.60 = (bf16[1,1024,256]{2,1,0:T(8,128)(2,1)}, bf16[1,1024,256]{2,1,0:T(8,128)(2,1)}) all-reduce(f32[1,1024,256]{2,1,0:T(8,128)} %get-tuple-element.1711, f32[1,1024,256]{2,1,0:T(8,128)} %get-tuple-element.1710), channel_id=1, replica_groups=mesh['dp'=8,'tensor'=4] {'tensor'}, use_global_device_ids=true, to_apply=%region_53.55 | all-reduce | flops 524288 | bytes 3145728 | tf_op jit(solution)/shard_map/psum | solution.py:214
  878.3 3.7 fusion.282
  897.8 4.1 convert_element_type.234
  909.5 29.1 %reduce-scatter.14.cloned.1.call-done = f32[1,1024,256]{2,1,0:T(8,128)} async-done(((f32[1,1024,1024]{2,1,0:T(8,128)}), f32[1,1024,256]{2,1,0:T(8,128)}) %reduce-scatter.14.cloned.1.call-update) | async-done | bytes 1048592 | tf_op jit(solution)/shard_map/reduce_scatter | solution.py:232
  941.6 17.2 %all-reduce.55 = (f32[1,1024]{1,0:T(1,128)S(1)}, f32[1,1024]{1,0:T(1,128)S(1)}, f32[4,256]{1,0:T(4,128)S(1)}, f32[256]{0:T(256)S(1)}) all-reduce(f32[1,1024]{1,0:T(1,128)S(1)} %bitcast.1478, f32[1,1024]{1,0:T(1,128)S(1)} %bitcast.1477, f32[4,256]{1,0:T(4,128)S(1)} %add_add_fusion.1, ...), channel_id=1, replica_groups=mesh['dp'=8,'tensor'=4] {'tensor'}, use_global_device_ids=true, to_apply=%region_55.57 | all-reduce | flops 3328 | bytes 26624 | tf_op jit(solution)/shard_map/psum | solution.py:233
  958.9 22.9 %all-reduce.54 = (f32[256]{0:T(256)}, f32[4,512]{1,0:T(4,128)}, f32[512]{0:T(512)}, f32[4,256]{1,0:T(4,128)}, f32[256]{0:T(256)}, /*index=5*/f32[8]{0:T(128)}, f32[8]{0:T(128)}, f32[8]{0:T(128)}, f32[512]{0:T(512)}) all-reduce(f32[256]{0:T(256)S(1)} %add.571, ...), channel_id=1, replica_groups=mesh['dp'=8,'tensor'=4] {'dp'}, use_global_device_ids=true, to_apply=%region_58.60 | all-reduce | flops 4632 | bytes 37056 | tf_op jit(solution)/shard_map/psum | solution.py:263
  985.9 27.5 %reduce-scatter.22.cloned.1.call-done = f32[128,256]{1,0:T(8,128)} async-done(((f32[1024,256]{1,0:T(8,128)}), f32[128,256]{1,0:T(8,128)}) %reduce-scatter.22.cloned.1.call-update) | async-done | bytes 131088 | tf_op jit(solution)/shard_map/reduce_scatter | solution.py:259
  1013.5 45.5 %reduce-scatter.26.cloned.1.call-done = f32[512,128]{1,0:T(8,128)} async-done(((f32[512,1024]{1,0:T(8,128)}), f32[512,128]{1,0:T(8,128)}) %reduce-scatter.26.cloned.1.call-update) | async-done | bytes 262160 | tf_op jit(solution)/shard_map/reduce_scatter | solution.py:261
  1058.9 45.0 %reduce-scatter.20.cloned.1.call-done = f32[128,512]{1,0:T(8,128)} async-done(((f32[1024,512]{1,0:T(8,128)}), f32[128,512]{1,0:T(8,128)}) %reduce-scatter.20.cloned.1.call-update) | async-done | bytes 262160 | tf_op jit(solution)/shard_map/reduce_scatter | solution.py:258
  1103.9 45.5 %reduce-scatter.18.cloned.1.call-done = f32[128,512]{1,0:T(8,128)} async-done(((f32[1024,512]{1,0:T(8,128)}), f32[128,512]{1,0:T(8,128)}) %reduce-scatter.18.cloned.1.call-update) | async-done | bytes 262160 | tf_op jit(solution)/shard_map/reduce_scatter | solution.py:257
  (1176 shorter events, 449.2 us)
Async XLA Ops:
  7.2 307.1 %copy-start = (bf16[1024,512]{1,0:T(8,128)(2,1)S(1)}, bf16[1024,512]{1,0:T(8,128)(2,1)}, u32[]{:S(2)}) copy-start(bf16[1024,512]{1,0:T(8,128)(2,1)} %param.30) | copy-start | bytes 3145732
  7.2 345.2 %all-gather.5.cloned.1.call-start = ((), (), s32[]{:S(2)}) async-start(), calls=%async_computation.13 | async-start | bytes 2621440 | tf_op jit(solution)/shard_map/all_gather | solution.py:178
  9.7 347.6 %all-gather.3.cloned.1.call-start = ((), (), s32[]{:S(2)}) async-start(), calls=%async_computation.11 | async-start | bytes 2621440 | tf_op jit(solution)/shard_map/all_gather | solution.py:178
  12.1 11.6 %copy-start.145 = (s32[2,1024]{1,0:T(2,128)S(1)}, s32[2,1024]{1,0:T(2,128)}, u32[]{:S(2)}) copy-start(s32[2,1024]{1,0:T(2,128)} %param.27) | copy-start | bytes 24580
  12.1 13.2 %copy-start.146 = (f32[4,512]{1,0:T(4,128)S(1)}, f32[4,512]{1,0:T(4,128)}, u32[]{:S(2)}) copy-start(f32[4,512]{1,0:T(4,128)} %param.34) | copy-start | bytes 24580
  12.1 43.5 %copy-start.150 = (f32[4,256]{1,0:T(4,128)S(1)}, f32[4,256]{1,0:T(4,128)}, u32[]{:S(2)}) copy-start(f32[4,256]{1,0:T(4,128)} %param.36) | copy-start | bytes 12292
  12.1 43.6 %copy-start.155 = (f32[8]{0:T(128)S(1)}, f32[8]{0:T(128)}, u32[]{:S(2)}) copy-start(f32[8]{0:T(128)} %param.39) | copy-start | bytes 100
  12.1 43.6 %copy-start.154 = (f32[8]{0:T(128)S(1)}, f32[8]{0:T(128)}, u32[]{:S(2)}) copy-start(f32[8]{0:T(128)} %param.40) | copy-start | bytes 100
  12.1 23.5 %collective-permute-start.3 = (bf16[1,1024,256]{2,1,0:T(8,128)(2,1)}, bf16[1,1024,256]{2,1,0:T(8,128)(2,1)}, u32[]{:S(2)}, u32[]{:S(2)}) collective-permute-start(bf16[1,1024,256]{2,1,0:T(8,128)(2,1)} %get-tuple-element.1657), channel_id=1, source_target_pairs={{0,1},{1,2},{2,3},{3,0},{4,5},{5,6},{6,7},{7,4},{8,9},{9,10},{10,1... | collective-permute-start | bytes 1572872 | tf_op jit(solution)/shard_map/ppermute | solution.py:20
  15.2 76.4 %collective-permute-start.4 = (bf16[1,1024,256]{2,1,0:T(8,128)(2,1)}, bf16[1,1024,256]{2,1,0:T(8,128)(2,1)}, u32[]{:S(2)}, u32[]{:S(2)}) collective-permute-start(bf16[1,1024,256]{2,1,0:T(8,128)(2,1)} %get-tuple-element.1657), channel_id=1, source_target_pairs={{0,3},{1,0},{2,1},{3,2},{4,7},{5,4},{6,5},{7,6},{8,11},{9,8},{10,9... | collective-permute-start | bytes 1572872 | tf_op jit(solution)/shard_map/ppermute | solution.py:23
  17.3 57.5 %collective-permute-start = (bf16[1,1024,256]{2,1,0:T(8,128)(2,1)}, bf16[1,1024,256]{2,1,0:T(8,128)(2,1)}, u32[]{:S(2)}, u32[]{:S(2)}) collective-permute-start(bf16[1,1024,256]{2,1,0:T(8,128)(2,1)} %get-tuple-element.1655), channel_id=1, source_target_pairs={{0,1},{1,2},{2,3},{3,0},{4,5},{5,6},{6,7},{7,4},{8,9},{9,10},{10,1... | collective-permute-start | bytes 1572872 | tf_op jit(solution)/shard_map/ppermute | solution.py:20
  17.3 79.8 %collective-permute-start.1 = (bf16[1,1024,256]{2,1,0:T(8,128)(2,1)}, bf16[1,1024,256]{2,1,0:T(8,128)(2,1)}, u32[]{:S(2)}, u32[]{:S(2)}) collective-permute-start(bf16[1,1024,256]{2,1,0:T(8,128)(2,1)} %get-tuple-element.1655), channel_id=1, source_target_pairs={{0,3},{1,0},{2,1},{3,2},{4,7},{5,4},{6,5},{7,6},{8,11},{9,8},{10,9... | collective-permute-start | bytes 1572872 | tf_op jit(solution)/shard_map/ppermute | solution.py:23
  21.1 883.8 %reduce-scatter.12.cloned.1.call-start = ((), (), s32[]{:S(2)}) async-start(), calls=%async_computation.10 | async-start | bytes 5242880 | tf_op jit(solution)/shard_map/reduce_scatter | solution.py:203
  25.2 116.7 %copy-start.82 = (f32[1,1024]{1,0:T(1,128)}, f32[1,1024]{1,0:T(1,128)S(1)}, u32[]{:S(2)}) copy-start(f32[1,1024]{1,0:T(1,128)S(1)} %get-tuple-element.1694) | copy-start | bytes 12292
  25.2 116.7 %copy-start.84 = (f32[1,1024]{1,0:T(1,128)}, f32[1,1024]{1,0:T(1,128)S(1)}, u32[]{:S(2)}) copy-start(f32[1,1024]{1,0:T(1,128)S(1)} %get-tuple-element.1695) | copy-start | bytes 12292
  25.2 116.7 %copy-start.86 = (f32[1,1024]{1,0:T(1,128)}, f32[1,1024]{1,0:T(1,128)S(1)}, u32[]{:S(2)}) copy-start(f32[1,1024]{1,0:T(1,128)S(1)} %get-tuple-element.1696) | copy-start | bytes 12292
  25.3 116.7 %copy-start.88 = (f32[1,1024]{1,0:T(1,128)}, f32[1,1024]{1,0:T(1,128)S(1)}, u32[]{:S(2)}) copy-start(f32[1,1024]{1,0:T(1,128)S(1)} %get-tuple-element.1720) | copy-start | bytes 12292
  25.3 116.7 %copy-start.90 = (f32[1,1024]{1,0:T(1,128)}, f32[1,1024]{1,0:T(1,128)S(1)}, u32[]{:S(2)}) copy-start(f32[1,1024]{1,0:T(1,128)S(1)} %get-tuple-element.1721) | copy-start | bytes 12292
  25.3 116.7 %copy-start.92 = (f32[1,1024]{1,0:T(1,128)}, f32[1,1024]{1,0:T(1,128)S(1)}, u32[]{:S(2)}) copy-start(f32[1,1024]{1,0:T(1,128)S(1)} %get-tuple-element.1722) | copy-start | bytes 12292
  25.3 116.7 %copy-start.123 = (f32[1,512]{1,0:T(1,128)}, f32[1,512]{1,0:T(1,128)S(1)}, u32[]{:S(2)}) copy-start(f32[1,512]{1,0:T(1,128)S(1)} %get-tuple-element.1670) | copy-start | bytes 6148
  25.3 116.7 %copy-start.125 = (f32[1,512]{1,0:T(1,128)}, f32[1,512]{1,0:T(1,128)S(1)}, u32[]{:S(2)}) copy-start(f32[1,512]{1,0:T(1,128)S(1)} %get-tuple-element.1671) | copy-start | bytes 6148
  25.3 116.7 %copy-start.127 = (f32[1,512]{1,0:T(1,128)}, f32[1,512]{1,0:T(1,128)S(1)}, u32[]{:S(2)}) copy-start(f32[1,512]{1,0:T(1,128)S(1)} %get-tuple-element.1672) | copy-start | bytes 6148
  25.3 116.7 %copy-start.129 = (f32[1,512]{1,0:T(1,128)}, f32[1,512]{1,0:T(1,128)S(1)}, u32[]{:S(2)}) copy-start(f32[1,512]{1,0:T(1,128)S(1)} %get-tuple-element.1673) | copy-start | bytes 6148
  35.6 73.4 %collective-permute-start.5 = (bf16[1,1024,256]{2,1,0:T(8,128)(2,1)}, bf16[1,1024,256]{2,1,0:T(8,128)(2,1)}, u32[]{:S(2)}, u32[]{:S(2)}) collective-permute-start(bf16[1,1024,256]{2,1,0:T(8,128)(2,1)} %collective-permute-done.3), channel_id=1, source_target_pairs={{0,1},{1,2},{2,3},{3,0},{4,5},{5,6},{6,7},{7,4},{8,9},{9,10},{10,1... | collective-permute-start | bytes 1572872 | tf_op jit(solution)/shard_map/ppermute | solution.py:20
  55.6 82.0 %copy-start.133 = (f32[1,256]{1,0:T(1,128)}, f32[1,256]{1,0:T(1,128)S(1)}, u32[]{:S(2)}) copy-start(f32[1,256]{1,0:T(1,128)S(1)} %get-tuple-element.1691) | copy-start | bytes 3076
  55.6 82.0 %copy-start.135 = (f32[1,256]{1,0:T(1,128)}, f32[1,256]{1,0:T(1,128)S(1)}, u32[]{:S(2)}) copy-start(f32[1,256]{1,0:T(1,128)S(1)} %get-tuple-element.1692) | copy-start | bytes 3076
  55.6 82.0 %copy-start.137 = (f32[1,256]{1,0:T(1,128)}, f32[1,256]{1,0:T(1,128)S(1)}, u32[]{:S(2)}) copy-start(f32[1,256]{1,0:T(1,128)S(1)} %get-tuple-element.1693) | copy-start | bytes 3076
  55.6 82.0 %copy-start.139 = (f32[1,256]{1,0:T(1,128)}, f32[1,256]{1,0:T(1,128)S(1)}, u32[]{:S(2)}) copy-start(f32[1,256]{1,0:T(1,128)S(1)} %get-tuple-element.1690) | copy-start | bytes 3076
  55.7 78.5 %copy-start.148 = (f32[8]{0:T(128)}, f32[8]{0:T(128)S(1)}, u32[]{:S(2)}) copy-start(f32[8]{0:T(128)S(1)} %exp.270) | copy-start | bytes 100
  55.9 261.5 %copy-start.119 = (f32[512]{0:T(512)}, f32[512]{0:T(512)S(1)}, u32[]{:S(2)}) copy-start(f32[512]{0:T(512)S(1)} %mul.2320) | copy-start | bytes 6148
  74.8 49.8 %collective-permute-start.2 = (bf16[1,1024,256]{2,1,0:T(8,128)(2,1)}, bf16[1,1024,256]{2,1,0:T(8,128)(2,1)S(1)}, u32[]{:S(2)}, u32[]{:S(2)}) collective-permute-start(bf16[1,1024,256]{2,1,0:T(8,128)(2,1)} %collective-permute-done), channel_id=1, source_target_pairs={{0,1},{1,2},{2,3},{3,0},{4,5},{5,6},{6,7},{7,4},{8,9},{9,10},{10,1... | collective-permute-start | bytes 1572872 | tf_op jit(solution)/shard_map/ppermute | solution.py:20
  113.1 12.9 %copy-start.147 = (f32[1024]{0:T(1024)S(1)}, f32[1024]{0:T(1024)}, u32[]{:S(2)}) copy-start(f32[1024]{0:T(1024)} %param.29) | copy-start | bytes 12292
  113.7 15.2 %copy-start.107 = (f32[1024]{0:T(1024)}, f32[1024]{0:T(1024)S(1)}, u32[]{:S(2)}) copy-start(f32[1024]{0:T(1024)S(1)} %get-tuple-element.1682) | copy-start | bytes 12292
  132.9 9.1 copy-start.9
  147.1 229.3 %copy-start.1 = (f32[1,1024,512]{2,1,0:T(8,128)}, f32[1,1024,512]{2,1,0:T(8,128)S(1)}, u32[]{:S(2)}) copy-start(f32[1,1024,512]{2,1,0:T(8,128)S(1)} %get-tuple-element.1592) | copy-start | bytes 6291460
  318.6 23.1 %copy-start.121 = (f32[512]{0:T(512)S(1)}, f32[512]{0:T(512)}, u32[]{:S(2)}) copy-start(f32[512]{0:T(512)} %param.41) | copy-start | bytes 6148
  341.7 34.7 %copy-start.103 = (f32[1,1024]{1,0:T(1,128)}, f32[1,1024]{1,0:T(1,128)S(1)}, u32[]{:S(2)}) copy-start(f32[1,1024]{1,0:T(1,128)S(1)} %add_rsqrt_fusion) | copy-start | bytes 12292
  346.8 558.1 %reduce-scatter.10.cloned.1.call-start = ((), (), s32[]{:S(2)}) async-start(), calls=%async_computation.9 | async-start | bytes 5242880 | tf_op jit(solution)/shard_map/reduce_scatter | solution.py:203
  347.1 29.3 %copy-start.111 = (f32[1024]{0:T(1024)}, f32[1024]{0:T(1024)S(1)}, u32[]{:S(2)}) copy-start(f32[1024]{0:T(1024)S(1)} %multiply_multiply_fusion.13) | copy-start | bytes 12292
  347.1 29.3 %copy-start.105 = (f32[1,1024]{1,0:T(1,128)}, f32[1,1024]{1,0:T(1,128)S(1)}, u32[]{:S(2)}) copy-start(f32[1,1024]{1,0:T(1,128)S(1)} %add_rsqrt_fusion.2) | copy-start | bytes 12292
  347.1 29.3 %copy-start.113 = (f32[1024]{0:T(1024)}, f32[1024]{0:T(1024)S(1)}, u32[]{:S(2)}) copy-start(f32[1024]{0:T(1024)S(1)} %multiply_multiply_fusion.15) | copy-start | bytes 12292
  352.3 555.5 %reduce-scatter.16.cloned.1.call-start = ((), (), s32[]{:S(2)}) async-start(), calls=%async_computation.14 | async-start | bytes 5242880 | tf_op jit(solution)/shard_map/reduce_scatter | solution.py:232
  400.3 10.9 copy-start.55
  433.5 10.9 copy-start.55
  466.5 10.9 copy-start.55
  499.7 10.9 copy-start.55
  546.3 12.2 %copy-start.56 = (f32[1,256,8]{1,2,0:T(8,128)}, f32[1,256,8]{1,2,0:T(8,128)S(1)}, u32[]{:S(2)}) copy-start(f32[1,256,8]{1,2,0:T(8,128)S(1)} %get-tuple-element.2217) | copy-start | bytes 24580 | tf_op jit(solution)/shard_map/transpose(jvp())/while
  565.0 8.8 copy-start.40
  581.3 12.2 %copy-start.56 = (f32[1,256,8]{1,2,0:T(8,128)}, f32[1,256,8]{1,2,0:T(8,128)S(1)}, u32[]{:S(2)}) copy-start(f32[1,256,8]{1,2,0:T(8,128)S(1)} %get-tuple-element.2217) | copy-start | bytes 24580 | tf_op jit(solution)/shard_map/transpose(jvp())/while
  600.1 8.8 copy-start.40
  616.3 12.2 %copy-start.56 = (f32[1,256,8]{1,2,0:T(8,128)}, f32[1,256,8]{1,2,0:T(8,128)S(1)}, u32[]{:S(2)}) copy-start(f32[1,256,8]{1,2,0:T(8,128)S(1)} %get-tuple-element.2217) | copy-start | bytes 24580 | tf_op jit(solution)/shard_map/transpose(jvp())/while
  635.1 8.8 copy-start.40
  651.4 12.2 %copy-start.56 = (f32[1,256,8]{1,2,0:T(8,128)}, f32[1,256,8]{1,2,0:T(8,128)S(1)}, u32[]{:S(2)}) copy-start(f32[1,256,8]{1,2,0:T(8,128)S(1)} %get-tuple-element.2217) | copy-start | bytes 24580 | tf_op jit(solution)/shard_map/transpose(jvp())/while
  670.1 8.8 copy-start.40
  727.6 211.1 %reduce-scatter.14.cloned.1.call-start = ((), (), s32[]{:S(2)}) async-start(), calls=%async_computation.12 | async-start | bytes 5242880 | tf_op jit(solution)/shard_map/reduce_scatter | solution.py:232
  735.4 250.5 %reduce-scatter.24.cloned.1.call-start = ((), (), s32[]{:S(2)}) async-start(), calls=%async_computation.18 | async-start | bytes 36864 | tf_op jit(solution)/shard_map/reduce_scatter | solution.py:260
  875.1 138.4 %reduce-scatter.22.cloned.1.call-start = ((), (), s32[]{:S(2)}) async-start(), calls=%async_computation.17 | async-start | bytes 1179648 | tf_op jit(solution)/shard_map/reduce_scatter | solution.py:259
  878.3 180.7 %reduce-scatter.26.cloned.1.call-start = ((), (), s32[]{:S(2)}) async-start(), calls=%async_computation.19 | async-start | bytes 2359296 | tf_op jit(solution)/shard_map/reduce_scatter | solution.py:261
  884.9 219.0 %reduce-scatter.20.cloned.1.call-start = ((), (), s32[]{:S(2)}) async-start(), calls=%async_computation.16 | async-start | bytes 2359296 | tf_op jit(solution)/shard_map/reduce_scatter | solution.py:258
  890.8 258.6 %reduce-scatter.18.cloned.1.call-start = ((), (), s32[]{:S(2)}) async-start(), calls=%async_computation.15 | async-start | bytes 2359296 | tf_op jit(solution)/shard_map/reduce_scatter | solution.py:257
  906.7 31.9 %copy-start.108 = (f32[1024]{0:T(1024)S(1)}, f32[1024]{0:T(1024)}, u32[]{:S(2)}) copy-start(f32[1024]{0:T(1024)} %copy-done.107) | copy-start | bytes 12292
  906.7 31.9 %copy-start.110 = (f32[1024]{0:T(1024)S(1)}, f32[1024]{0:T(1024)}, u32[]{:S(2)}) copy-start(f32[1024]{0:T(1024)} %copy-done.109) | copy-start | bytes 12292
  909.5 72.3 %copy-start.131 = (f32[1024]{0:T(1024)S(1)}, f32[1024]{0:T(1024)}, u32[]{:S(2)}) copy-start(f32[1024]{0:T(1024)} %get-tuple-element.1681) | copy-start | bytes 12292
  909.5 72.3 %copy-start.132 = (f32[1024]{0:T(1024)S(1)}, f32[1024]{0:T(1024)}, u32[]{:S(2)}) copy-start(f32[1024]{0:T(1024)} %get-tuple-element.1679) | copy-start | bytes 12292
  (216 other events, 898.8 us)
Sparse Core Ops, SparseCore 0:
  9.8 84.8 all-gather.4
  96.3 59.7 all-gather.2
  346.9 77.0 reduce-scatter.11
  426.3 77.2 reduce-scatter.9
  727.7 130.9 reduce-scatter.15
  860.9 77.6 reduce-scatter.13
  942.2 31.0 reduce-scatter.23
  977.4 36.0 reduce-scatter.21
  1017.7 41.2 reduce-scatter.25
  1062.7 41.2 reduce-scatter.19
  1108.1 41.2 reduce-scatter.17
